TPU v7x, 32 devices: a whole 2x2x4 slice. The times are simulated.
32 devices in a mesh: ens: 8 (over y, x, core), lat: 4 (over z).
Axes of the slice: x: 2, y: 2, z: 4, core: 2. Of those that a mesh axis runs over, the one named last changes fastest.
Arguments:
- ensemble: float32 [32, 3, 2, 256, 1440], P('ens', None, None, 'lat'), may hold values from -6 to 6
- ancestors: int32 [32], P('ens'), may hold values from 0 to 31, as said below
- depth: float32 [2, 256, 1440], P(None, 'lat'), may hold values from 0.3 to 1
- forcing: bfloat16 [32, 3, 2, 256, 1440], P('ens', None, None, 'lat'), may hold values from -4 to 4
Outputs:
- forecast: float32 [32, 3, 2, 256, 1440], P('ens', None, None, 'lat')
Inputs may be any that keep to these rules, and one draw needn't show every extreme that they name: The ancestors of particles g * 4 to (g + 1) * 4 - 1 lie among the last half of 4 particles of group g - 1, the 4 particles of group g and the first half of 4 particles of group g + 1, groups counted cyclically; every group takes at least one ancestor from each of its two neighbouring groups, and in every draw one group takes all its ancestors from its two neighbouring groups.
All inputs are finite; a program needn't handle non-finite values.
Results may differ from a plain program's by a relative error of at most 0.0003.
Values sent between devices are 32-bit elements; how exact they have to be, the bound alone decides.
A program may use at most 128 MiB of HBM per device.

v0:
```python
import jax
import jax.numpy as jnp
from jax import lax
from jax.sharding import PartitionSpec as P

SUBSTEPS = 3


time_step = 0.6
coriolis_peak = 0.5
reduced_gravity = 0.5


def from_behind(block, axis, distance):
    devices = range(lax.axis_size(axis))
    route = [((i - distance) % len(devices), i) for i in devices]
    return lax.ppermute(block, axis, route)


def with_halo(value, sides, width):
    for axis, dim in sides:
        peers, length = (lax.axis_size(axis), value.shape[dim])
        up = [(i, (i + 1) % peers) for i in range(peers - 1)]
        down = [(j, i) for i, j in up]
        last = lax.slice_in_dim(value, length - width, length, axis=dim)
        initial = lax.slice_in_dim(value, 0, width, axis=dim)
        before = lax.ppermute(last, axis, up)
        after = lax.ppermute(initial, axis, down)
        value = jnp.concatenate([before, value, after], axis=dim)
    return value


def layer_pressure(height, layer_axis):
    layers_here = height.shape[layer_axis]
    shape_ones = [1] * height.ndim
    shape_ones[layer_axis] = layers_here
    weights = (jnp.arange(layers_here) >= 1).astype(height.dtype).reshape(shape_ones)
    lowered = jnp.cumsum(height * weights, axis=layer_axis)
    return jnp.sum(height, axis=layer_axis, keepdims=True) + reduced_gravity * lowered


def coriolis_rows(first_row, count, total_rows):
    row_values = (first_row + jnp.arange(count)).astype(jnp.float32)
    latitude = jnp.pi * ((row_values + 0.5) / total_rows - 0.5)
    return coriolis_peak * jnp.sin(latitude)


def advance(padded, depth_ext, band_index, band_rows, total_rows):
    height = padded[:, 0]
    eastward = padded[:, 1]
    northward = padded[:, 2]
    flux_east = depth_ext * eastward
    flux_north = depth_ext * northward
    inner_flux = flux_east[:, :, 1 : band_rows + 3]
    divergence = (jnp.roll(inner_flux, -1, -1) - jnp.roll(inner_flux, 1, -1)) * 0.5 + (
        flux_north[:, :, 2 : band_rows + 4] - flux_north[:, :, 0 : band_rows + 2]
    ) * 0.5
    height_next = height[:, :, 1 : band_rows + 3] - time_step * divergence
    global_row = band_index * band_rows - 1 + jnp.arange(band_rows + 2)
    inside = ((global_row >= 0) & (global_row < total_rows)).astype(jnp.float32)[:, None]
    height_next = height_next * inside
    pressure = layer_pressure(height_next, 1)
    middle = pressure[:, :, 1 : band_rows + 1]
    slope_east = (jnp.roll(middle, -1, -1) - jnp.roll(middle, 1, -1)) * 0.5
    slope_north = (pressure[:, :, 2 : band_rows + 2] - pressure[:, :, 0:band_rows]) * 0.5
    east_inner = eastward[:, :, 2 : band_rows + 2]
    north_inner = northward[:, :, 2 : band_rows + 2]
    coriolis = coriolis_rows(band_index * band_rows, band_rows, total_rows)[:, None]
    east_next = east_inner + time_step * (coriolis * north_inner - slope_east)
    north_next = north_inner + time_step * (-coriolis * east_next - slope_north)
    return jnp.stack([height_next[:, :, 1 : band_rows + 1], east_next, north_next], axis=1)


def add_forcing(particle_state, forcing_now):
    return particle_state.at[:, 0].add(forcing_now.astype(jnp.float32))


def on_device(ensemble, ancestors, depth, forcing):
    part_dev = ensemble.shape[0]
    half_group = part_dev // 2
    band_rows = ensemble.shape[3]
    total_rows = band_rows * lax.axis_size("lat")
    total_parts = part_dev * lax.axis_size("ens")
    band_index = lax.axis_index("lat")
    group_index = lax.axis_index("ens")
    position = jnp.mod(ancestors - group_index * part_dev + half_group, total_parts)
    lower_half = from_behind(ensemble[part_dev - half_group :], "ens", 1)
    upper_half = from_behind(ensemble[:half_group], "ens", -1)
    depth_wide = depth[None, None]
    window = jnp.concatenate([lower_half, ensemble, upper_half], axis=0)
    chosen = jnp.take(window, position, axis=0)
    padded, depth_padded = (
        with_halo(chosen, (("lat", 3),), 2),
        with_halo(depth_wide, (("lat", 3),), 2),
    )
    depth_ext = depth_padded[0, 0]
    current = advance(padded, depth_ext, band_index, band_rows, total_rows)
    current = add_forcing(current, forcing[:, 0])
    for substep in range(1, SUBSTEPS):
        padded = with_halo(current, (("lat", 3),), 2)
        current = advance(padded, depth_ext, band_index, band_rows, total_rows)
        current = add_forcing(current, forcing[:, substep])
    return current


def solution(mesh):
    in_specs = (
        P("ens", None, None, "lat", None),
        P("ens"),
        P(None, "lat", None),
        P("ens", None, None, "lat", None),
    )
    out_specs = P("ens", None, None, "lat", None)
    return jax.shard_map(
        on_device, mesh=mesh, in_specs=in_specs, out_specs=out_specs, check_vma=False
    )
```

profile of v0, /device:TPU:0, one launch (start us, length us, event | category | flops | bytes accessed | tf_op | source)
XLA Modules:
  0.0 305.1 jit_solution(14082110595451547529)
XLA Ops:
  0.0 8.9 %fusion.59 = (f32[2,3,2,64,1440]{4,3,2,1,0:T(8,128)}, f32[2,3,2,64,1440]{4,3,2,1,0:T(8,128)}) fusion(f32[4,3,2,64,1440]{4,3,2,1,0:T(8,128)} %param.10), kind=kLoop, calls=%fused_computation.111 | loop fusion | bytes 17694720 | tf_op jit(solution)/shard_map/slice | solution.py:87
  12.2 4.2 %collective-permute-start.4 = (f32[1,1,2,2,1440]{4,3,2,1,0:T(2,128)S(1)}, f32[1,1,2,2,1440]{4,3,2,1,0:T(2,128)S(1)}, u32[]{:S(2)}, u32[]{:S(2)}) collective-permute-start(f32[1,1,2,2,1440]{4,3,2,1,0:T(2,128)S(1)} %get-tuple-element.102), channel_id=1, source_target_pairs={{0,1},{1,2},{2,3},{4,5},{5,6},{6,7},{8,9},{9,10},{10,11},{12,13},{... | collective-permute-start | bytes 69128 | tf_op jit(solution)/shard_map/ppermute | solution.py:27
  17.9 94.3 %collective-permute-done = f32[2,3,2,64,1440]{4,3,2,1,0:T(8,128)} collective-permute-done((f32[2,3,2,64,1440]{4,3,2,1,0:T(8,128)}, f32[2,3,2,64,1440]{4,3,2,1,0:T(8,128)}, u32[]{:S(2)}, u32[]{:S(2)}) %collective-permute-start) | collective-permute-done | bytes 4423712 | tf_op jit(solution)/shard_map/ppermute | solution.py:17
  113.7 13.7 %pad_maximum_fusion = f32[8,3,2,64,1440]{4,3,2,1,0:T(8,128)} fusion(f32[2,3,2,64,1440]{4,3,2,1,0:T(8,128)} %collective-permute-done.1, f32[4,3,2,64,1440]{4,3,2,1,0:T(8,128)} %param.10, f32[2,3,2,64,1440]{4,3,2,1,0:T(8,128)} %collective-permute-done), kind=kLoop, calls=%fused_computation.1 | loop fusion | flops 8847360 | bytes 35389440 | tf_op jit(solution)/shard_map/concatenate | solution.py:90
  127.4 11.3 %gather_fusion = f32[4,3,2,64,1440]{4,3,2,1,0:T(8,128)} fusion(f32[8,3,2,64,1440]{4,3,2,1,0:T(8,128)} %pad_maximum_fusion, s32[1024]{0:T(1024)S(1)} %pad_clamp_fusion), kind=kCustom, calls=%fused_computation | custom fusion | bytes 17694736 | tf_op jit(solution)/shard_map/jit(_take)/gather | solution.py:91
  138.7 4.8 %broadcast_select_fusion = f32[4,3,2,64,1440]{4,3,2,1,0:T(8,128)S(1)} fusion(f32[4,3,2,64,1440]{4,3,2,1,0:T(8,128)} %gather_fusion, pred[4]{0:T(512)(128)(4,1)S(1)} %get-tuple-element.53), kind=kLoop, calls=%fused_computation.8 | loop fusion | flops 2211840 | bytes 17694724 | tf_op jit(solution)/shard_map/jit(_take)/select_n | solution.py:91
  148.9 5.0 %collective-permute-done.2 = f32[4,3,2,2,1440]{4,3,2,1,0:T(2,128)S(1)} collective-permute-done((f32[4,3,2,2,1440]{4,3,2,1,0:T(2,128)S(1)}, f32[4,3,2,2,1440]{4,3,2,1,0:T(2,128)S(1)}, u32[]{:S(2)}, u32[]{:S(2)}) %collective-permute-start.2) | collective-permute-done | bytes 276512 | tf_op jit(solution)/shard_map/ppermute | solution.py:27
  153.9 4.7 %collective-permute-done.3 = f32[4,3,2,2,1440]{4,3,2,1,0:T(2,128)S(1)} collective-permute-done((f32[4,3,2,2,1440]{4,3,2,1,0:T(2,128)S(1)}, f32[4,3,2,2,1440]{4,3,2,1,0:T(2,128)S(1)}, u32[]{:S(2)}, u32[]{:S(2)}) %collective-permute-start.3) | collective-permute-done | bytes 276512 | tf_op jit(solution)/shard_map/ppermute | solution.py:28
  158.6 5.7 %pad_maximum_fusion.1 = f32[4,3,2,68,1440]{4,3,2,1,0:T(8,128)S(1)} fusion(f32[4,3,2,2,1440]{4,3,2,1,0:T(2,128)S(1)} %collective-permute-done.3, f32[4,3,2,64,1440]{4,3,2,1,0:T(8,128)} %copy-done.2, f32[4,3,2,2,1440]{4,3,2,1,0:T(2,128)S(1)} %collective-permute-done.2), kind=kLoop, calls=%fused_computation.2 | loop fusion | flops 4700160 | bytes 18800640 | tf_op jit(solution)/shard_map/concatenate | solution.py:29
  164.3 4.2 %slice_bitcast_fusion.7 = (f32[4,2,68,1440]{3,2,1,0:T(8,128)}, f32[4,2,68,1440]{3,2,1,0:T(8,128)}, f32[4,2,68,1440]{3,2,1,0:T(8,128)}) fusion(f32[4,3,2,68,1440]{4,3,2,1,0:T(8,128)S(1)} %pad_maximum_fusion.1), kind=kLoop, calls=%fused_computation.34 | loop fusion | bytes 18800640 | tf_op jit(solution)/shard_map/squeeze | solution.py:50
  184.0 5.2 %fusion.29 = (f32[4,1,2,64,1440]{4,3,2,0,1:T(8,128)S(1)}, f32[4,2,64,1440]{3,2,1,0:T(8,128)}) fusion(f32[4,2,66,1440]{3,2,1,0:T(8,128)S(1)} %broadcast_add_fusion.2, f32[4,2,68,1440]{3,2,1,0:T(8,128)S(1)} %copy-done.10, f32[64]{0:T(128)S(1)} %get-tuple-element.105, f32[4,2,64,1439]{3,2,1,0:T(8,128)} %get-tuple-element.95, ...), kind=kLoop, calls=%fused_computation.63 | loop fusion | flops 10321920 | bytes 23593472 | tf_op jit(solution)/shard_map/stack | solution.py:71
  199.7 5.2 %collective-permute-done.6 = f32[4,3,2,2,1440]{4,3,2,0,1:T(2,128)S(1)} collective-permute-done((f32[4,3,2,2,1440]{4,3,2,0,1:T(2,128)S(1)}, f32[4,3,2,2,1440]{4,3,2,0,1:T(2,128)S(1)}, u32[]{:S(2)}, u32[]{:S(2)}) %collective-permute-start.6) | collective-permute-done | bytes 276512 | tf_op jit(solution)/shard_map/ppermute | solution.py:27
  204.8 4.1 %collective-permute-done.7 = f32[4,3,2,2,1440]{4,3,2,0,1:T(2,128)S(1)} collective-permute-done((f32[4,3,2,2,1440]{4,3,2,0,1:T(2,128)S(1)}, f32[4,3,2,2,1440]{4,3,2,0,1:T(2,128)S(1)}, u32[]{:S(2)}, u32[]{:S(2)}) %collective-permute-start.7) | collective-permute-done | bytes 276512 | tf_op jit(solution)/shard_map/ppermute | solution.py:28
  209.0 5.7 %pad_maximum_fusion.2 = f32[4,3,2,68,1440]{4,3,2,0,1:T(8,128)S(1)} fusion(f32[4,3,2,2,1440]{4,3,2,0,1:T(2,128)S(1)} %collective-permute-done.7, f32[4,3,2,64,1440]{4,3,2,0,1:T(8,128)} %copy-done, f32[4,3,2,2,1440]{4,3,2,0,1:T(2,128)S(1)} %collective-permute-done.6), kind=kLoop, calls=%fused_computation.3 | loop fusion | flops 4700160 | bytes 18800640 | tf_op jit(solution)/shard_map/concatenate | solution.py:29
  218.7 4.3 %slice_bitcast_fusion.4 = (f32[4,2,68,1440]{3,2,1,0:T(8,128)}, f32[4,2,68,1440]{3,2,1,0:T(8,128)}, f32[4,2,68,1440]{3,2,1,0:T(8,128)}) fusion(f32[4,3,2,68,1440]{4,3,2,0,1:T(8,128)S(1)} %pad_maximum_fusion.2), kind=kLoop, calls=%fused_computation.26 | loop fusion | bytes 18800640 | tf_op jit(solution)/shard_map/squeeze | solution.py:50
  224.1 4.9 %fusion.66 = (f32[4,2,66,1439]{3,2,1,0:T(8,128)S(1)}, f32[4,2,66,1439]{3,2,1,0:T(8,128)S(1)}) fusion(f32[4,2,68,1440]{3,2,1,0:T(8,128)} %get-tuple-element.57), kind=kLoop, calls=%fused_computation.118 | loop fusion | bytes 12156672 | tf_op jit(solution)/shard_map/jit(_roll_static)/slice | solution.py:55
  238.4 5.2 %fusion.24 = (f32[4,1,2,64,1440]{4,3,2,0,1:T(8,128)S(1)}, f32[4,2,64,1440]{3,2,1,0:T(8,128)}) fusion(f32[4,2,66,1440]{3,2,1,0:T(8,128)S(1)} %broadcast_add_fusion.1, f32[4,2,68,1440]{3,2,1,0:T(8,128)S(1)} %copy-done.14, f32[64]{0:T(128)S(1)} %get-tuple-element.105, f32[4,2,64,1439]{3,2,1,0:T(8,128)} %get-tuple-element.87, ...), kind=kLoop, calls=%fused_computation.55 | loop fusion | flops 10321920 | bytes 23593472 | tf_op jit(solution)/shard_map/stack | solution.py:71
  254.1 4.0 %collective-permute-done.8 = f32[4,3,2,2,1440]{4,3,2,0,1:T(2,128)S(1)} collective-permute-done((f32[4,3,2,2,1440]{4,3,2,0,1:T(2,128)S(1)}, f32[4,3,2,2,1440]{4,3,2,0,1:T(2,128)S(1)}, u32[]{:S(2)}, u32[]{:S(2)}) %collective-permute-start.8) | collective-permute-done | bytes 276512 | tf_op jit(solution)/shard_map/ppermute | solution.py:27
  258.1 4.1 %collective-permute-done.9 = f32[4,3,2,2,1440]{4,3,2,0,1:T(2,128)S(1)} collective-permute-done((f32[4,3,2,2,1440]{4,3,2,0,1:T(2,128)S(1)}, f32[4,3,2,2,1440]{4,3,2,0,1:T(2,128)S(1)}, u32[]{:S(2)}, u32[]{:S(2)}) %collective-permute-start.9) | collective-permute-done | bytes 276512 | tf_op jit(solution)/shard_map/ppermute | solution.py:28
  262.2 5.7 %pad_maximum_fusion.3 = f32[4,3,2,68,1440]{4,3,2,0,1:T(8,128)S(1)} fusion(f32[4,3,2,2,1440]{4,3,2,0,1:T(2,128)S(1)} %collective-permute-done.9, f32[4,3,2,64,1440]{4,3,2,0,1:T(8,128)} %copy-done.1, f32[4,3,2,2,1440]{4,3,2,0,1:T(2,128)S(1)} %collective-permute-done.8), kind=kLoop, calls=%fused_computation.4 | loop fusion | flops 4700160 | bytes 18800640 | tf_op jit(solution)/shard_map/concatenate | solution.py:29
  271.9 4.3 %slice_bitcast_fusion.1 = (f32[4,2,68,1440]{3,2,1,0:T(8,128)}, f32[4,2,68,1440]{3,2,1,0:T(8,128)}, f32[4,2,68,1440]{3,2,1,0:T(8,128)}) fusion(f32[4,3,2,68,1440]{4,3,2,0,1:T(8,128)S(1)} %pad_maximum_fusion.3), kind=kLoop, calls=%fused_computation.18 | loop fusion | bytes 18800640 | tf_op jit(solution)/shard_map/squeeze | solution.py:50
  277.4 4.9 %fusion.62 = (f32[4,2,66,1439]{3,2,1,0:T(8,128)S(1)}, f32[4,2,66,1439]{3,2,1,0:T(8,128)S(1)}) fusion(f32[4,2,68,1440]{3,2,1,0:T(8,128)} %get-tuple-element.55), kind=kLoop, calls=%fused_computation.114 | loop fusion | bytes 12156672 | tf_op jit(solution)/shard_map/jit(_roll_static)/slice | solution.py:55
  291.6 4.1 %fusion.19 = (f32[4,1,2,64,1440]{4,3,2,0,1:T(8,128)S(1)}, f32[4,2,64,1440]{3,2,1,0:T(8,128)S(1)}) fusion(f32[4,2,66,1440]{3,2,1,0:T(8,128)S(1)} %broadcast_add_fusion, f32[4,2,68,1440]{3,2,1,0:T(8,128)S(1)} %copy-done.12, f32[64]{0:T(128)S(1)} %get-tuple-element.105, f32[4,2,64,1439]{3,2,1,0:T(8,128)} %get-tuple-element.79, ...), kind=kLoop, calls=%fused_computation.47 | loop fusion | flops 10321920 | bytes 23593472 | tf_op jit(solution)/shard_map/stack | solution.py:71
  300.0 4.6 %copy.13 = f32[4,3,2,64,1440]{4,3,2,1,0:T(8,128)} copy(f32[4,3,2,64,1440]{4,3,2,0,1:T(8,128)S(1)} %add_dynamic-update-slice_fusion) | data formatting | bytes 17694720 | tf_op jit(solution)/shard_map/scatter-add | solution.py:75
  (84 shorter events, 81.1 us)
Async XLA Ops:
  0.0 12.2 %copy-start.15 = (f32[2,64,1440]{2,1,0:T(8,128)S(1)}, f32[2,64,1440]{2,1,0:T(8,128)}, u32[]{:S(2)}) copy-start(f32[2,64,1440]{2,1,0:T(8,128)} %param.12) | copy-start | bytes 2211844
  0.0 17.8 %copy-start.16 = (s32[4]{0:T(128)S(1)}, s32[4]{0:T(128)}, u32[]{:S(2)}) copy-start(s32[4]{0:T(128)} %param.11) | copy-start | bytes 52
  8.9 103.3 %collective-permute-start = (f32[2,3,2,64,1440]{4,3,2,1,0:T(8,128)}, f32[2,3,2,64,1440]{4,3,2,1,0:T(8,128)}, u32[]{:S(2)}, u32[]{:S(2)}) collective-permute-start(f32[2,3,2,64,1440]{4,3,2,1,0:T(8,128)} %get-tuple-element.76), channel_id=1, source_target_pairs={{28,0},{0,4},{4,8},{8,12},{12,16},{16,20},{20,24},{24,28},{29,1},{... | collective-permute-start | bytes 13271048 | tf_op jit(solution)/shard_map/ppermute | solution.py:17
  9.3 104.4 %collective-permute-start.1 = (f32[2,3,2,64,1440]{4,3,2,1,0:T(8,128)}, f32[2,3,2,64,1440]{4,3,2,1,0:T(8,128)}, u32[]{:S(2)}, u32[]{:S(2)}) collective-permute-start(f32[2,3,2,64,1440]{4,3,2,1,0:T(8,128)} %get-tuple-element.77), channel_id=1, source_target_pairs={{4,0},{8,4},{12,8},{16,12},{20,16},{24,20},{28,24},{0,28},{5,1},{9... | collective-permute-start | bytes 13271048 | tf_op jit(solution)/shard_map/ppermute | solution.py:17
  12.2 136.5 %collective-permute-start.4 = (f32[1,1,2,2,1440]{4,3,2,1,0:T(2,128)S(1)}, f32[1,1,2,2,1440]{4,3,2,1,0:T(2,128)S(1)}, u32[]{:S(2)}, u32[]{:S(2)}) collective-permute-start(f32[1,1,2,2,1440]{4,3,2,1,0:T(2,128)S(1)} %get-tuple-element.102), channel_id=1, source_target_pairs={{0,1},{1,2},{2,3},{4,5},{5,6},{6,7},{8,9},{9,10},{10,11},{12,13},{... | collective-permute-start | bytes 69128 | tf_op jit(solution)/shard_map/ppermute | solution.py:27
  16.5 132.3 %collective-permute-start.5 = (f32[1,1,2,2,1440]{4,3,2,1,0:T(2,128)S(1)}, f32[1,1,2,2,1440]{4,3,2,1,0:T(2,128)S(1)}, u32[]{:S(2)}, u32[]{:S(2)}) collective-permute-start(f32[1,1,2,2,1440]{4,3,2,1,0:T(2,128)S(1)} %get-tuple-element.103), channel_id=1, source_target_pairs={{1,0},{2,1},{3,2},{5,4},{6,5},{7,6},{9,8},{10,9},{11,10},{13,12},{... | collective-permute-start | bytes 69128 | tf_op jit(solution)/shard_map/ppermute | solution.py:28
  143.5 10.3 %copy-start.2 = (f32[4,3,2,64,1440]{4,3,2,1,0:T(8,128)}, f32[4,3,2,64,1440]{4,3,2,1,0:T(8,128)S(1)}, u32[]{:S(2)}) copy-start(f32[4,3,2,64,1440]{4,3,2,1,0:T(8,128)S(1)} %broadcast_select_fusion) | copy-start | bytes 26542084
  143.8 10.1 %collective-permute-start.2 = (f32[4,3,2,2,1440]{4,3,2,1,0:T(2,128)S(1)}, f32[4,3,2,2,1440]{4,3,2,1,0:T(2,128)S(1)}, u32[]{:S(2)}, u32[]{:S(2)}) collective-permute-start(f32[4,3,2,2,1440]{4,3,2,1,0:T(2,128)S(1)} %get-tuple-element.74), channel_id=1, source_target_pairs={{0,1},{1,2},{2,3},{4,5},{5,6},{6,7},{8,9},{9,10},{10,11},{12,13},{... | collective-permute-start | bytes 829448 | tf_op jit(solution)/shard_map/ppermute | solution.py:27
  147.3 11.3 %collective-permute-start.3 = (f32[4,3,2,2,1440]{4,3,2,1,0:T(2,128)S(1)}, f32[4,3,2,2,1440]{4,3,2,1,0:T(2,128)S(1)}, u32[]{:S(2)}, u32[]{:S(2)}) collective-permute-start(f32[4,3,2,2,1440]{4,3,2,1,0:T(2,128)S(1)} %get-tuple-element.75), channel_id=1, source_target_pairs={{1,0},{2,1},{3,2},{5,4},{6,5},{7,6},{9,8},{10,9},{11,10},{13,12},{... | collective-permute-start | bytes 829448 | tf_op jit(solution)/shard_map/ppermute | solution.py:28
  179.8 3.1 %copy-start.9 = (f32[4,2,68,1440]{3,2,1,0:T(8,128)S(1)}, f32[4,2,68,1440]{3,2,1,0:T(8,128)}, u32[]{:S(2)}) copy-start(f32[4,2,68,1440]{3,2,1,0:T(8,128)} %get-tuple-element.67) | copy-start | bytes 9400324
  179.8 4.2 %copy-start.10 = (f32[4,2,68,1440]{3,2,1,0:T(8,128)S(1)}, f32[4,2,68,1440]{3,2,1,0:T(8,128)}, u32[]{:S(2)}) copy-start(f32[4,2,68,1440]{3,2,1,0:T(8,128)} %get-tuple-element.69) | copy-start | bytes 9400324
  194.4 10.4 %copy-start = (f32[4,3,2,64,1440]{4,3,2,0,1:T(8,128)}, f32[4,3,2,64,1440]{4,3,2,0,1:T(8,128)S(1)}, u32[]{:S(2)}) copy-start(f32[4,3,2,64,1440]{4,3,2,0,1:T(8,128)S(1)} %add_dynamic-update-slice_fusion.2) | copy-start | bytes 26542084
  194.7 10.2 %collective-permute-start.6 = (f32[4,3,2,2,1440]{4,3,2,0,1:T(2,128)S(1)}, f32[4,3,2,2,1440]{4,3,2,0,1:T(2,128)S(1)}, u32[]{:S(2)}, u32[]{:S(2)}) collective-permute-start(f32[4,3,2,2,1440]{4,3,2,0,1:T(2,128)S(1)} %get-tuple-element.72), channel_id=1, source_target_pairs={{0,1},{1,2},{2,3},{4,5},{5,6},{6,7},{8,9},{9,10},{10,11},{12,13},{... | collective-permute-start | bytes 829448 | tf_op jit(solution)/shard_map/ppermute | solution.py:27
  198.2 10.8 %collective-permute-start.7 = (f32[4,3,2,2,1440]{4,3,2,0,1:T(2,128)S(1)}, f32[4,3,2,2,1440]{4,3,2,0,1:T(2,128)S(1)}, u32[]{:S(2)}, u32[]{:S(2)}) collective-permute-start(f32[4,3,2,2,1440]{4,3,2,0,1:T(2,128)S(1)} %get-tuple-element.73), channel_id=1, source_target_pairs={{1,0},{2,1},{3,2},{5,4},{6,5},{7,6},{9,8},{10,9},{11,10},{13,12},{... | collective-permute-start | bytes 829448 | tf_op jit(solution)/shard_map/ppermute | solution.py:28
  224.1 4.9 %copy-start.4 = (f32[4,2,68,1440]{3,2,1,0:T(8,128)S(1)}, f32[4,2,68,1440]{3,2,1,0:T(8,128)}, u32[]{:S(2)}) copy-start(f32[4,2,68,1440]{3,2,1,0:T(8,128)} %get-tuple-element.58) | copy-start | bytes 9400324
  224.1 5.1 %copy-start.8 = (f32[4,2,68,1440]{3,2,1,0:T(8,128)S(1)}, f32[4,2,68,1440]{3,2,1,0:T(8,128)}, u32[]{:S(2)}) copy-start(f32[4,2,68,1440]{3,2,1,0:T(8,128)} %get-tuple-element.66) | copy-start | bytes 9400324
  234.2 3.1 %copy-start.13 = (f32[4,2,68,1440]{3,2,1,0:T(8,128)S(1)}, f32[4,2,68,1440]{3,2,1,0:T(8,128)}, u32[]{:S(2)}) copy-start(f32[4,2,68,1440]{3,2,1,0:T(8,128)} %get-tuple-element.64) | copy-start | bytes 9400324
  234.2 4.2 %copy-start.14 = (f32[4,2,68,1440]{3,2,1,0:T(8,128)S(1)}, f32[4,2,68,1440]{3,2,1,0:T(8,128)}, u32[]{:S(2)}) copy-start(f32[4,2,68,1440]{3,2,1,0:T(8,128)} %get-tuple-element.65) | copy-start | bytes 9400324
  248.8 9.3 %copy-start.1 = (f32[4,3,2,64,1440]{4,3,2,0,1:T(8,128)}, f32[4,3,2,64,1440]{4,3,2,0,1:T(8,128)S(1)}, u32[]{:S(2)}) copy-start(f32[4,3,2,64,1440]{4,3,2,0,1:T(8,128)S(1)} %add_dynamic-update-slice_fusion.1) | copy-start | bytes 26542084
  249.0 9.0 %collective-permute-start.8 = (f32[4,3,2,2,1440]{4,3,2,0,1:T(2,128)S(1)}, f32[4,3,2,2,1440]{4,3,2,0,1:T(2,128)S(1)}, u32[]{:S(2)}, u32[]{:S(2)}) collective-permute-start(f32[4,3,2,2,1440]{4,3,2,0,1:T(2,128)S(1)} %get-tuple-element.70), channel_id=1, source_target_pairs={{0,1},{1,2},{2,3},{4,5},{5,6},{6,7},{8,9},{9,10},{10,11},{12,13},{... | collective-permute-start | bytes 829448 | tf_op jit(solution)/shard_map/ppermute | solution.py:27
  252.5 9.7 %collective-permute-start.9 = (f32[4,3,2,2,1440]{4,3,2,0,1:T(2,128)S(1)}, f32[4,3,2,2,1440]{4,3,2,0,1:T(2,128)S(1)}, u32[]{:S(2)}, u32[]{:S(2)}) collective-permute-start(f32[4,3,2,2,1440]{4,3,2,0,1:T(2,128)S(1)} %get-tuple-element.71), channel_id=1, source_target_pairs={{1,0},{2,1},{3,2},{5,4},{6,5},{7,6},{9,8},{10,9},{11,10},{13,12},{... | collective-permute-start | bytes 829448 | tf_op jit(solution)/shard_map/ppermute | solution.py:28
  277.4 4.9 %copy-start.3 = (f32[4,2,68,1440]{3,2,1,0:T(8,128)S(1)}, f32[4,2,68,1440]{3,2,1,0:T(8,128)}, u32[]{:S(2)}) copy-start(f32[4,2,68,1440]{3,2,1,0:T(8,128)} %get-tuple-element.56) | copy-start | bytes 9400324
  277.4 5.1 %copy-start.7 = (f32[4,2,68,1440]{3,2,1,0:T(8,128)S(1)}, f32[4,2,68,1440]{3,2,1,0:T(8,128)}, u32[]{:S(2)}) copy-start(f32[4,2,68,1440]{3,2,1,0:T(8,128)} %get-tuple-element.63) | copy-start | bytes 9400324
  287.4 4.2 %copy-start.12 = (f32[4,2,68,1440]{3,2,1,0:T(8,128)S(1)}, f32[4,2,68,1440]{3,2,1,0:T(8,128)}, u32[]{:S(2)}) copy-start(f32[4,2,68,1440]{3,2,1,0:T(8,128)} %get-tuple-element.62) | copy-start | bytes 9400324
  (3 other events, 8.2 us)
where the time goes:
time: 309 us; the launch traced here: 305 us
  waiting for transfers between devices  123 us (40%)
  other arithmetic  84 us (27%)
  local copies, waits for them, and re-layouts  73.4 us (24%)
  starting transfers between devices  23.8 us (8%)
    ppermute x2, waiting for transfers between devices, from_behind(): return lax.ppermute(block, axis, route)  95.9 us
    another operation x6, other arithmetic, advance(): jnp.stack([height_next[:, :, 1:band_rows + 1], east_next, north_next], ax...  23.1 us
    concatenate x3, other arithmetic, with_halo(): value = jnp.concatenate([before, value, after], axis=dim)  17.2 us
    ppermute x4, starting transfers between devices, with_halo(): before = lax.ppermute(last, axis, up)  14.7 us
    ppermute x4, waiting for transfers between devices, with_halo(): before = lax.ppermute(last, axis, up)  14.1 us
    slice x6, local copies, waits for them, and re-layouts, advance(): jnp.roll(inner_flux, -1, -1) - jnp.roll(inner_flux, 1, -1)  13.9 us
    concatenate x1, other arithmetic, on_device(): window = jnp.concatenate([lower_half, ensemble, upper_half], axis=0)  13.7 us
    ppermute x4, waiting for transfers between devices, with_halo(): after = lax.ppermute(initial, axis, down)  13 us
  transfers between devices with their start and end apart: 10, of which 8 were waited for; matrix products, arithmetic and copies ran while one was open for 10% of the time, Pallas kernels for 0%

commit v1 on v0

v1 whole, which is shorter than its diff:
```python
import functools

import jax
import jax.numpy as jnp
from jax import lax
from jax.experimental import pallas as pl
from jax.experimental.pallas import tpu as pltpu
from jax.sharding import PartitionSpec as P

SUBSTEPS = 3
time_step = 0.6
coriolis_peak = 0.5
reduced_gravity = 0.5

EDGE = 8
MESH = pl.DeviceIdType.MESH


def coriolis_rows(first_row, count, total_rows):
    row_values = (first_row + jnp.arange(count)).astype(jnp.float32)
    latitude = jnp.pi * ((row_values + 0.5) / total_rows - 0.5)
    return coriolis_peak * jnp.sin(latitude)


def exchange(
    n_ens, n_lat, own, depth, force_lo, force_hi,
    recv, halo_lo, halo_hi, depth_lo, depth_hi, edge_lo, edge_hi,
    send_sem, recv_sem, lat_send, lat_recv,
):
    ens, lat = lax.axis_index("ens"), lax.axis_index("lat")
    nxt, prv = lax.rem(ens + 1, n_ens), lax.rem(ens + n_ens - 1, n_ens)
    part_dev, rows = own.shape[0], own.shape[3]
    half = part_dev // 2
    has_lo, has_hi = lat > 0, lat < n_lat - 1

    barrier = pltpu.get_barrier_semaphore()
    pl.semaphore_signal(barrier, inc=1, device_id=(nxt, lat), device_id_type=MESH)
    pl.semaphore_signal(barrier, inc=1, device_id=(prv, lat), device_id_type=MESH)

    @pl.when(has_lo)
    def _():
        pl.semaphore_signal(barrier, inc=1, device_id=(ens, lat - 1), device_id_type=MESH)

    @pl.when(has_hi)
    def _():
        pl.semaphore_signal(barrier, inc=1, device_id=(ens, lat + 1), device_id_type=MESH)

    pl.semaphore_wait(barrier, 2 + jnp.where(has_lo, 1, 0) + jnp.where(has_hi, 1, 0))

    pieces = ((0, EDGE), (rows - EDGE, EDGE), (EDGE, rows - 2 * EDGE))

    def ens_copies(i):
        at = pl.ds(*pieces[i])
        up = pltpu.make_async_remote_copy(
            src_ref=own.at[pl.ds(half, half), :, :, at, :],
            dst_ref=recv.at[pl.ds(0, half), :, :, at, :],
            send_sem=send_sem.at[2 * i], recv_sem=recv_sem.at[2 * i],
            device_id=(nxt, lat), device_id_type=MESH,
        )
        down = pltpu.make_async_remote_copy(
            src_ref=own.at[pl.ds(0, half), :, :, at, :],
            dst_ref=recv.at[pl.ds(half, half), :, :, at, :],
            send_sem=send_sem.at[2 * i + 1], recv_sem=recv_sem.at[2 * i + 1],
            device_id=(prv, lat), device_id_type=MESH,
        )
        return up, down

    copies = [ens_copies(i) for i in range(3)]
    for pair in copies:
        for c in pair:
            c.start()

    def lat_copies(side):
        at = pl.ds(rows - EDGE, EDGE) if side == 0 else pl.ds(0, EDGE)
        halo, dep, edge = ((halo_lo, depth_lo, edge_lo), (halo_hi, depth_hi, edge_hi))[side]
        force = (force_hi, force_lo)[side]
        pairs = (
            (own.at[:, :, :, at, :], halo.at[pl.ds(half, part_dev)]),
            (depth.at[:, at, :], dep),
            (force, edge),
            (recv.at[pl.ds(0, half), :, :, at, :], halo.at[pl.ds(0, half)]),
            (recv.at[pl.ds(half, half), :, :, at, :], halo.at[pl.ds(half + part_dev, half)]),
        )
        to = (ens, lat + 1) if side == 0 else (ens, lat - 1)
        return [
            pltpu.make_async_remote_copy(
                src_ref=s, dst_ref=d, send_sem=lat_send.at[5 * side + j], recv_sem=lat_recv.at[5 * side + j],
                device_id=to, device_id_type=MESH,
            )
            for j, (s, d) in enumerate(pairs)
        ]

    to_hi, to_lo = lat_copies(0), lat_copies(1)

    @pl.when(has_hi)
    def _():
        for c in to_hi[:3]:
            c.start()

    @pl.when(has_lo)
    def _():
        for c in to_lo[:3]:
            c.start()

    for c in (*copies[0], *copies[1]):
        c.wait_recv()

    @pl.when(has_hi)
    def _():
        for c in to_hi[3:]:
            c.start()

    @pl.when(has_lo)
    def _():
        for c in to_lo[3:]:
            c.start()

    for c in copies[2]:
        c.wait_recv()

    @pl.when(has_hi)
    def _():
        for c in to_hi:
            c.wait_send()
        for c in to_lo:
            c.wait_recv()

    @pl.when(has_lo)
    def _():
        for c in to_lo:
            c.wait_send()
        for c in to_hi:
            c.wait_recv()

    for pair in copies:
        for c in pair:
            c.wait_send()


def substeps(
    n_lat, position, own, recv, halo_lo, halo_hi, depth, depth_lo, depth_hi, forcing, edge_lo, edge_hi, coriolis,
    out, raw, state, press, deep, force, sems,
):
    p = pl.program_id(0)
    parts = pl.num_programs(0)
    lat = lax.axis_index("lat")
    half = recv.shape[0] // 2
    part_dev, rows, lon = own.shape[0], own.shape[3], own.shape[4]
    wide = state.shape[3]
    layers = own.shape[2]
    blocks = (rows + 2 * EDGE) // 8
    total = n_lat * rows

    def fetch(q, slot, act):
        w = position[q]
        body = raw.at[slot, :, :, pl.ds(EDGE, rows), :]

        def go(src, dst, j):
            c = pltpu.make_async_copy(src, dst, sems.at[slot, j])
            (c.start if act else c.wait)()

        if act:
            @pl.when(w < half)
            def _():
                go(recv.at[w], body, 0)

            @pl.when((w >= half) & (w < half + part_dev))
            def _():
                go(own.at[w - half], body, 0)

            @pl.when(w >= half + part_dev)
            def _():
                go(recv.at[w - part_dev], body, 0)
        else:
            go(own.at[0], body, 0)
        go(halo_lo.at[w], raw.at[slot, :, :, pl.ds(0, EDGE), :], 1)
        go(halo_hi.at[w], raw.at[slot, :, :, pl.ds(EDGE + rows, EDGE), :], 2)

    slot = lax.rem(p, 2)

    @pl.when(p == 0)
    def _():
        fetch(0, 0, True)

    @pl.when(p + 1 < parts)
    def _():
        fetch(p + 1, 1 - slot, True)

    lane = lax.broadcasted_iota(jnp.int32, (8, 128), 1)
    row = lax.broadcasted_iota(jnp.int32, (8, wide), 0)
    inside_lo, inside_hi = lat > 0, lat < n_lat - 1
    tail = (lon // 128) * 128
    left = lon - tail

    def put(ref, index, at, value):
        ref[(*index, at, pl.ds(0, lon))] = value
        last = ref[(*index, at, pl.ds(tail, 128))]
        first = ref[(*index, at, pl.ds(0, 128))]
        ref[(*index, at, pl.ds(tail, 128))] = jnp.where(
            lane < left,
            last,
            jnp.where(lane < 128 - left, pltpu.roll(first, left, 1), pltpu.roll(last, 128 - left, 1)),
        )

    def at_block(e):
        return pl.ds(pl.multiple_of(e * 8, 8), 8)

    @pl.when(p == 0)
    def _():
        for k in range(layers):
            put(deep, (k,), pl.ds(0, 8), jnp.where(inside_lo, depth_lo[k], 0.0))
            put(deep, (k,), pl.ds(EDGE + rows, 8), jnp.where(inside_hi, depth_hi[k], 0.0))

            @pl.loop(0, rows // 8)
            def _(e):
                put(deep, (k,), at_block(e + 1), depth[k, at_block(e), :])

    for s in range(SUBSTEPS):
        for k in range(layers):
            if s < SUBSTEPS - 1:
                put(force, (s, k), pl.ds(0, 8), jnp.where(inside_lo, edge_lo[0, s, k], 0.0))
                put(force, (s, k), pl.ds(EDGE + rows, 8), jnp.where(inside_hi, edge_hi[0, s, k], 0.0))
            else:
                force[s, k, pl.ds(0, 8), :] = jnp.zeros((8, wide), jnp.float32)
                force[s, k, pl.ds(EDGE + rows, 8), :] = jnp.zeros((8, wide), jnp.float32)

            @pl.loop(0, rows // 16)
            def _(e):
                both = forcing[0, s, k, pl.ds(pl.multiple_of(e * 16, 16), 16), :].astype(jnp.float32)
                put(force, (s, k), at_block(2 * e + 1), both[:8])
                put(force, (s, k), at_block(2 * e + 2), both[8:])

    fetch(p, slot, False)

    @pl.loop(0, blocks)
    def _(e):
        inside = ((e > 0) | inside_lo) & ((e < blocks - 1) | inside_hi)
        for f in range(3):
            for k in range(layers):
                put(state, (f, k), at_block(e), jnp.where(inside, raw[slot, f, k, at_block(e), :], 0.0))

    def from_below(before, here):
        return pltpu.roll(jnp.where(row == 7, before, here), 1, 0)

    def from_above(after, here):
        return pltpu.roll(jnp.where(row == 0, after, here), 7, 0)

    for s in range(SUBSTEPS):

        @pl.loop(0, blocks)
        def _(e):
            here, before, after = at_block(e), at_block(jnp.maximum(e - 1, 0)), at_block(jnp.minimum(e + 1, blocks - 1))
            inside = ((e > 0) | inside_lo) & ((e < blocks - 1) | inside_hi)
            heights = []
            for k in range(layers):
                east = deep[k, here, :] * state[1, k, here, :]
                north = deep[k, here, :] * state[2, k, here, :]
                below = from_below(deep[k, before, :] * state[2, k, before, :], north)
                above = from_above(deep[k, after, :] * state[2, k, after, :], north)
                divergence = (pltpu.roll(east, wide - 1, 1) - pltpu.roll(east, 1, 1)) * 0.5 + (above - below) * 0.5
                height = state[0, k, here, :] - time_step * divergence
                heights.append(height)
                state[0, k, here, :] = height + force[s, k, here, :]
            base = functools.reduce(jnp.add, heights)
            lowered = jnp.zeros_like(base)
            for k in range(layers):
                if k:
                    lowered = lowered + heights[k]
                press[k, here, :] = jnp.where(inside, base + reduced_gravity * lowered, 0.0)

        final = s == SUBSTEPS - 1

        @pl.loop(1 if final else 0, blocks - 1 if final else blocks)
        def _(e):
            here, before, after = at_block(e), at_block(jnp.maximum(e - 1, 0)), at_block(jnp.minimum(e + 1, blocks - 1))
            inside = ((e > 0) | inside_lo) & ((e < blocks - 1) | inside_hi)
            turn = jnp.concatenate([coriolis[here, :]] * (wide // 128), axis=1)
            for k in range(layers):
                mid = press[k, here, :]
                slope_east = (pltpu.roll(mid, wide - 1, 1) - pltpu.roll(mid, 1, 1)) * 0.5
                slope_north = (from_above(press[k, after, :], mid) - from_below(press[k, before, :], mid)) * 0.5
                north = state[2, k, here, :]
                east_next = state[1, k, here, :] + time_step * (turn * north - slope_east)
                north_next = north + time_step * (-turn * east_next - slope_north)
                if final:
                    to = at_block(e - 1)
                    out[0, 0, k, to, :] = state[0, k, here, :][:, :lon]
                    out[0, 1, k, to, :] = east_next[:, :lon]
                    out[0, 2, k, to, :] = north_next[:, :lon]
                else:
                    state[1, k, here, :] = jnp.where(inside, east_next, 0.0)
                    state[2, k, here, :] = jnp.where(inside, north_next, 0.0)


def on_device(n_ens, n_lat, ensemble, ancestors, depth, forcing):
    part_dev, fields, layers, rows, lon = ensemble.shape
    half = part_dev // 2
    f32 = jnp.float32
    wide = -(-lon // 128) * 128
    any_space = pl.BlockSpec(memory_space=pl.ANY)
    force_lo = forcing[:, : SUBSTEPS - 1, :, :EDGE].astype(f32)
    force_hi = forcing[:, : SUBSTEPS - 1, :, rows - EDGE :].astype(f32)
    halo = jax.ShapeDtypeStruct((2 * part_dev, fields, layers, EDGE, lon), f32)
    depth_edge = jax.ShapeDtypeStruct((layers, EDGE, lon), f32)
    force_edge = jax.ShapeDtypeStruct(force_lo.shape, f32)
    recv, halo_lo, halo_hi, depth_lo, depth_hi, edge_lo, edge_hi = pl.pallas_call(
        functools.partial(exchange, n_ens, n_lat),
        out_shape=(
            jax.ShapeDtypeStruct(ensemble.shape, f32), halo, halo, depth_edge, depth_edge, force_edge, force_edge,
        ),
        in_specs=[any_space] * 4,
        out_specs=(any_space,) * 7,
        scratch_shapes=[
            pltpu.SemaphoreType.DMA((6,)), pltpu.SemaphoreType.DMA((6,)),
            pltpu.SemaphoreType.DMA((10,)), pltpu.SemaphoreType.DMA((10,)),
        ],
        compiler_params=pltpu.CompilerParams(collective_id=0, has_side_effects=True),
        name="exchange",
    )(ensemble, depth, force_lo, force_hi)

    total = part_dev * n_ens
    position = jnp.mod(ancestors - lax.axis_index("ens") * part_dev + half, total)
    turn = coriolis_rows(lax.axis_index("lat") * rows - EDGE, rows + 2 * EDGE, rows * n_lat)
    turn = jnp.broadcast_to(turn[:, None], (rows + 2 * EDGE, 128))
    padded = rows + 2 * EDGE

    def whole(shape):
        return pl.BlockSpec(shape, lambda p, *_: (0,) * len(shape))

    return pl.pallas_call(
        functools.partial(substeps, n_lat),
        out_shape=jax.ShapeDtypeStruct(ensemble.shape, f32),
        grid_spec=pltpu.PrefetchScalarGridSpec(
            num_scalar_prefetch=1,
            grid=(part_dev,),
            in_specs=[
                any_space, any_space, any_space, any_space,
                whole(depth.shape), whole(depth_edge.shape), whole(depth_edge.shape),
                pl.BlockSpec((1, SUBSTEPS, layers, rows, lon), lambda p, *_: (p, 0, 0, 0, 0)),
                pl.BlockSpec((1, *force_edge.shape[1:]), lambda p, *_: (p, 0, 0, 0, 0)),
                pl.BlockSpec((1, *force_edge.shape[1:]), lambda p, *_: (p, 0, 0, 0, 0)),
                whole(turn.shape),
            ],
            out_specs=pl.BlockSpec((1, fields, layers, rows, lon), lambda p, *_: (p, 0, 0, 0, 0)),
            scratch_shapes=[
                pltpu.VMEM((2, fields, layers, padded, lon), f32),
                pltpu.VMEM((fields, layers, padded, wide), f32),
                pltpu.VMEM((layers, padded, wide), f32),
                pltpu.VMEM((layers, padded, wide), f32),
                pltpu.VMEM((SUBSTEPS, layers, padded, wide), f32),
                pltpu.SemaphoreType.DMA((2, 3)),
            ],
        ),
        compiler_params=pltpu.CompilerParams(vmem_limit_bytes=56 * 2**20),
        name="substeps",
    )(
        position, ensemble, recv, halo_lo, halo_hi, depth, depth_lo, depth_hi, forcing, edge_lo, edge_hi, turn
    )


def solution(mesh):
    in_specs = (
        P("ens", None, None, "lat", None),
        P("ens"),
        P(None, "lat", None),
        P("ens", None, None, "lat", None),
    )
    out_specs = P("ens", None, None, "lat", None)
    return jax.shard_map(
        functools.partial(on_device, mesh.shape["ens"], mesh.shape["lat"]),
        mesh=mesh, in_specs=in_specs, out_specs=out_specs, check_vma=False,
    )
```

time: 309 us -> 170 us (0.55); the launches traced: 305 us -> 169 us
  Pallas kernels: 0 us -> 165 us
  waiting for transfers between devices: 123 us -> 0 us
  other arithmetic: 84 us -> 3.78 us
  local copies, waits for them, and re-layouts: 73.4 us -> 0.69 us
  starting transfers between devices: 23.8 us -> 0 us
    pallas_call x0 -> x2, Pallas kernels: none -> 165 us  [the longest x1 106 us: on_device(): pl.pallas_call(functools.partial(exchange, n_ens, n_lat), out_shape=(jax....]
    ppermute x10 -> x0, waiting for transfers between devices: 123 us -> none  [the longest x2 95.9 us: from_behind(): return lax.ppermute(block, axis, route)]
    slice x17 -> x0, local copies, waits for them, and re-layouts: 33.1 us -> none  [the longest x6 13.9 us: advance(): jnp.roll(inner_flux, -1, -1) - jnp.roll(inner_flux, 1, -1)]
    concatenate x4 -> x0, other arithmetic: 30.9 us -> none  [the longest x3 17.2 us: with_halo(): value = jnp.concatenate([before, value, after], axis=dim)]
    another operation x9 -> x0, other arithmetic: 24.6 us -> none  [the longest x6 23.1 us: advance(): jnp.stack([height_next[:, :, 1:band_rows + 1], east_next, north_next], ax...]
    ppermute x10 -> x0, starting transfers between devices: 23.8 us -> none  [the longest x4 14.7 us: with_halo(): before = lax.ppermute(last, axis, up)]
    squeeze x3 -> x0, local copies, waits for them, and re-layouts: 12.7 us -> none  [advance(): eastward = padded[:, 1]]
    gather x1 -> x0, local copies, waits for them, and re-layouts: 11.3 us -> none  [on_device(): chosen = jnp.take(window, position, axis=0)]
  transfers between devices with their start and end apart: 10 -> 0, of which waited for: 8 -> 0; matrix products, arithmetic and copies ran while one was open for 10% -> 0% of each run, Pallas kernels for 0% -> 0%
where the time goes in v1:
time: 170 us; the launch traced here: 169 us
  Pallas kernels  165 us (97%)
  other arithmetic  3.78 us (2%)
    pallas_call x1, Pallas kernels, on_device(): pl.pallas_call(functools.partial(exchange, n_ens, n_lat), out_shape=(jax....  106 us
    pallas_call x1, Pallas kernels, on_device(): pl.pallas_call(functools.partial(substeps, n_lat), out_shape=jax.ShapeDty...  58.5 us

profile of v1, /device:TPU:0, one launch (start us, length us, event | category | flops | bytes accessed | tf_op | source)
XLA Modules:
  0.0 169.4 jit_solution(16527701817750758378)
XLA Ops:
  0.0 1.3 and_select_fusion.position
  1.3 0.7 broadcast_in_dim.2.coriolis
  2.0 2.5 %slice_convert_fusion = (f32[4,2,2,8,1440]{4,3,2,1,0:T(8,128)}, f32[4,2,2,8,1440]{4,3,2,1,0:T(8,128)}) fusion(bf16[4,3,2,64,1440]{4,3,2,1,0:T(8,128)(2,1)} %forcing.1), kind=kLoop, calls=%fused_computation | loop fusion | flops 368640 | bytes 2211840 | tf_op jit(solution)/shard_map/convert_element_type | solution.py:302
  4.5 106.5 %exchange.1 = (f32[4,3,2,64,1440]{4,3,2,1,0:T(8,128)}, f32[8,3,2,8,1440]{4,3,2,1,0:T(8,128)}, f32[8,3,2,8,1440]{4,3,2,1,0:T(8,128)}, f32[2,8,1440]{2,1,0:T(8,128...) custom-call(f32[4,3,2,64,1440]{4,3,2,1,0:T(8,128)} %own.3, ...), custom_call_target="tpu_custom_call" | custom-call | tf_op jit(solution)/shard_map/exchange/pallas_call | solution.py:306
  110.9 58.5 %substeps.1 = f32[4,3,2,64,1440]{4,3,2,1,0:T(8,128)} custom-call(s32[4]{0:T(128)} %and_select_fusion.position, f32[4,3,2,64,1440]{4,3,2,1,0:T(8,128)} %own.3, f32[4,3,2,64,1440]{4,3,2,1,0:T(8,128)} %get-tuple-element.12.recv, f32[8,3,2,8,1440]{4,3,2,1,0:T(8,128)} %get-tuple-element.13.halo_lo, f32[8,3,2,8,1440]{4,3,2,1,0:T(8,128)} %get-tuple-element.14.halo_hi, ...), custom_call_target="tpu_custom_call" | custom-call | tf_op jit(solution)/shard_map/substeps/pallas_call | solution.py:330
  (1 shorter events, 0.0 us)

commit v2 on v0

v2 whole, which is shorter than its diff:
```python
import functools

import jax
import jax.numpy as jnp
from jax import lax
from jax.experimental import pallas as pl
from jax.experimental.pallas import tpu as pltpu
from jax.sharding import PartitionSpec as P

SUBSTEPS = 3
time_step = 0.6
coriolis_peak = 0.5
reduced_gravity = 0.5

EDGE = 8
MESH = pl.DeviceIdType.MESH


def coriolis_rows(first_row, count, total_rows):
    row_values = (first_row + jnp.arange(count)).astype(jnp.float32)
    latitude = jnp.pi * ((row_values + 0.5) / total_rows - 0.5)
    return coriolis_peak * jnp.sin(latitude)


def forecast_kernel(n_ens, n_lat, *refs):
    own, ancestors, depth, forcing, coriolis, out = refs[:6]
    rows, lon = own.shape[3], own.shape[4]
    chunks = rows // 8
    win = refs[6 : 6 + chunks]
    (
        state, press, deep, force, force_raw, depth_raw, stage_out,
        send_sem, recv_sem, own_sem, raw_sem, lat_send, lat_recv, out_sem,
    ) = refs[6 + chunks :]
    ens, lat = lax.axis_index("ens"), lax.axis_index("lat")
    nxt, prv = lax.rem(ens + 1, n_ens), lax.rem(ens + n_ens - 1, n_ens)
    part_dev, layers = own.shape[0], own.shape[2]
    half = part_dev // 2
    wide = state.shape[4]
    blocks = chunks + 2
    has_lo, has_hi = lat > 0, lat < n_lat - 1

    barrier = pltpu.get_barrier_semaphore()
    pl.semaphore_signal(barrier, inc=1, device_id=(nxt, lat), device_id_type=MESH)
    pl.semaphore_signal(barrier, inc=1, device_id=(prv, lat), device_id_type=MESH)

    @pl.when(has_lo)
    def _():
        pl.semaphore_signal(barrier, inc=1, device_id=(ens, lat - 1), device_id_type=MESH)

    @pl.when(has_hi)
    def _():
        pl.semaphore_signal(barrier, inc=1, device_id=(ens, lat + 1), device_id_type=MESH)

    pl.semaphore_wait(barrier, 2 + jnp.where(has_lo, 1, 0) + jnp.where(has_hi, 1, 0))

    def ens_copies(c):
        at = pl.ds(8 * c, 8)
        up = pltpu.make_async_remote_copy(
            src_ref=own.at[pl.ds(half, half), :, :, at, :], dst_ref=win[c].at[pl.ds(0, half)],
            send_sem=send_sem.at[2 * c], recv_sem=recv_sem.at[2 * c],
            device_id=(nxt, lat), device_id_type=MESH,
        )
        down = pltpu.make_async_remote_copy(
            src_ref=own.at[pl.ds(0, half), :, :, at, :], dst_ref=win[c].at[pl.ds(half + part_dev, half)],
            send_sem=send_sem.at[2 * c + 1], recv_sem=recv_sem.at[2 * c + 1],
            device_id=(prv, lat), device_id_type=MESH,
        )
        return up, down

    def own_copy(c):
        return pltpu.make_async_copy(
            own.at[:, :, :, pl.ds(8 * c, 8), :], win[c].at[pl.ds(half, part_dev)], own_sem.at[c]
        )

    order = (0, chunks - 1, *range(1, chunks - 1))
    for c in order:
        for copy in ens_copies(c):
            copy.start()
    depth_copy = pltpu.make_async_copy(depth, depth_raw, raw_sem.at[0])
    force_copy = pltpu.make_async_copy(forcing, force_raw, raw_sem.at[1])
    depth_copy.start()
    force_copy.start()
    for c in order:
        own_copy(c).start()

    lane = lax.broadcasted_iota(jnp.int32, (8, 128), 1)
    row = lax.broadcasted_iota(jnp.int32, (8, wide), 0)
    tail = (lon // 128) * 128
    left = lon - tail

    def put(ref, index, at, value):
        ref[(*index, at, pl.ds(0, lon))] = value
        last = ref[(*index, at, pl.ds(tail, 128))]
        first = ref[(*index, at, pl.ds(0, 128))]
        ref[(*index, at, pl.ds(tail, 128))] = jnp.where(
            lane < left,
            last,
            jnp.where(lane < 128 - left, pltpu.roll(first, left, 1), pltpu.roll(last, 128 - left, 1)),
        )

    def at_block(e):
        return pl.ds(pl.multiple_of(e * 8, 8), 8)

    top, bottom = pl.ds(0, 8), pl.ds(EDGE + rows, 8)
    first, last = pl.ds(8, 8), pl.ds(rows, 8)
    zero = jnp.zeros((8, wide), jnp.float32)

    def clear(at):
        for k in range(layers):
            deep[k, at, :] = zero

            @pl.loop(0, part_dev)
            def _(p):
                for s in range(SUBSTEPS - 1):
                    force[p, s, k, at, :] = zero
                for f in range(3):
                    state[p, f, k, at, :] = zero

    @pl.when(jnp.logical_not(has_lo))
    def _():
        clear(top)

    @pl.when(jnp.logical_not(has_hi))
    def _():
        clear(bottom)

    def lat_copies(side):
        src, dst = ((last, top), (first, bottom))[side]
        to = (ens, lat + 1) if side == 0 else (ens, lat - 1)
        pairs = (
            (deep.at[:, src, :], deep.at[:, dst, :]),
            (force.at[:, pl.ds(0, SUBSTEPS - 1), :, src, :], force.at[:, pl.ds(0, SUBSTEPS - 1), :, dst, :]),
            (state.at[:, :, :, src, :], state.at[:, :, :, dst, :]),
        )
        return [
            pltpu.make_async_remote_copy(
                src_ref=s, dst_ref=d, send_sem=lat_send.at[3 * side + j], recv_sem=lat_recv.at[3 * side + j],
                device_id=to, device_id_type=MESH,
            )
            for j, (s, d) in enumerate(pairs)
        ]

    to_hi, to_lo = lat_copies(0), lat_copies(1)

    def lat_start(lo, hi):
        @pl.when(has_hi)
        def _():
            for c in to_hi[lo:hi]:
                c.start()

        @pl.when(has_lo)
        def _():
            for c in to_lo[lo:hi]:
                c.start()

    depth_copy.wait()

    @pl.loop(0, chunks)
    def _(c):
        for k in range(layers):
            put(deep, (k,), at_block(c + 1), depth_raw[k, at_block(c), :])

    force_copy.wait()

    @pl.loop(0, part_dev)
    def _(p):
        for s in range(SUBSTEPS):
            for k in range(layers):
                if s == SUBSTEPS - 1:
                    force[p, s, k, top, :] = zero
                    force[p, s, k, bottom, :] = zero

                @pl.loop(0, rows // 16)
                def _(e):
                    both = force_raw[p, s, k, pl.ds(pl.multiple_of(e * 16, 16), 16), :].astype(jnp.float32)
                    put(force, (p, s, k), at_block(2 * e + 1), both[:8])
                    put(force, (p, s, k), at_block(2 * e + 2), both[8:])

    lat_start(0, 2)

    def take(c):
        for copy in ens_copies(c):
            copy.wait_recv()
        own_copy(c).wait()

        @pl.loop(0, part_dev)
        def _(p):
            w = lax.rem(ancestors[p] - ens * part_dev + half + n_ens * part_dev, n_ens * part_dev)
            w = jnp.minimum(w, 2 * part_dev - 1)
            for f in range(3):
                for k in range(layers):
                    put(state, (p, f, k), pl.ds(8 * c + 8, 8), win[c][w, f, k, :, :])

    take(0)
    take(chunks - 1)
    lat_start(2, 3)

    @pl.when(has_hi)
    def _():
        for c in to_hi:
            c.wait_send()
        for c in to_lo:
            c.wait_recv()

    @pl.when(has_lo)
    def _():
        for c in to_lo:
            c.wait_send()
        for c in to_hi:
            c.wait_recv()

    def from_below(before, here):
        return pltpu.roll(jnp.where(row == 7, before, here), 1, 0)

    def from_above(after, here):
        return pltpu.roll(jnp.where(row == 0, after, here), 7, 0)

    def around(e):
        inside = ((e > 0) | has_lo) & ((e < blocks - 1) | has_hi)
        return at_block(e), at_block(jnp.maximum(e - 1, 0)), at_block(jnp.minimum(e + 1, blocks - 1)), inside

    def heights_of(p, s, e):
        here, before, after, inside = around(e)
        heights = []
        for k in range(layers):
            east = deep[k, here, :] * state[p, 1, k, here, :]
            north = deep[k, here, :] * state[p, 2, k, here, :]
            below = from_below(deep[k, before, :] * state[p, 2, k, before, :], north)
            above = from_above(deep[k, after, :] * state[p, 2, k, after, :], north)
            divergence = (pltpu.roll(east, wide - 1, 1) - pltpu.roll(east, 1, 1)) * 0.5 + (above - below) * 0.5
            height = state[p, 0, k, here, :] - time_step * divergence
            heights.append(height)
            state[p, 0, k, here, :] = height + force[p, s, k, here, :]
        base = functools.reduce(jnp.add, heights)
        lowered = jnp.zeros_like(base)
        for k in range(layers):
            if k:
                lowered = lowered + heights[k]
            press[p, k, here, :] = jnp.where(inside, base + reduced_gravity * lowered, 0.0)

    def velocities(p, e, final):
        here, before, after, inside = around(e)
        turn = jnp.concatenate([coriolis[here, :]] * (wide // 128), axis=1)
        slot = lax.rem(e, 2)
        for k in range(layers):
            mid = press[p, k, here, :]
            slope_east = (pltpu.roll(mid, wide - 1, 1) - pltpu.roll(mid, 1, 1)) * 0.5
            slope_north = (from_above(press[p, k, after, :], mid) - from_below(press[p, k, before, :], mid)) * 0.5
            north = state[p, 2, k, here, :]
            east_next = state[p, 1, k, here, :] + time_step * (turn * north - slope_east)
            north_next = north + time_step * (-turn * east_next - slope_north)
            if final:
                stage_out[slot, p, 0, k, :, :] = state[p, 0, k, here, :][:, :lon]
                stage_out[slot, p, 1, k, :, :] = east_next[:, :lon]
                stage_out[slot, p, 2, k, :, :] = north_next[:, :lon]
            else:
                state[p, 1, k, here, :] = jnp.where(inside, east_next, 0.0)
                state[p, 2, k, here, :] = jnp.where(inside, north_next, 0.0)

    def out_copy(e):
        slot = lax.rem(e, 2)
        return pltpu.make_async_copy(stage_out.at[slot], out.at[:, :, :, at_block(e - 1), :], out_sem.at[slot])

    @pl.loop(0, blocks + 2 * SUBSTEPS - 2)
    def _(step):
        for c in range(1, chunks - 1):

            @pl.when(step == c)
            def _():
                take(c)

        @pl.loop(0, SUBSTEPS)
        def _(s):
            e = step - 2 * s

            @pl.when((e >= 0) & (e < blocks))
            def _():
                @pl.loop(0, part_dev)
                def _(p):
                    heights_of(p, s, e)

            j = e - 1

            @pl.when((j >= 0) & (j < blocks) & (s < SUBSTEPS - 1))
            def _():
                @pl.loop(0, part_dev)
                def _(p):
                    velocities(p, j, False)

        j = step - 2 * SUBSTEPS + 1

        @pl.when((j >= 1) & (j < blocks - 1))
        def _():
            @pl.when(j >= 3)
            def _():
                out_copy(j - 2).wait()

            @pl.loop(0, part_dev)
            def _(p):
                velocities(p, j, True)

            out_copy(j).start()

    out_copy(blocks - 3).wait()
    out_copy(blocks - 2).wait()
    for c in order:
        for copy in ens_copies(c):
            copy.wait_send()


def on_device(n_ens, n_lat, ensemble, ancestors, depth, forcing):
    part_dev, fields, layers, rows, lon = ensemble.shape
    f32 = jnp.float32
    wide = -(-lon // 128) * 128
    padded = rows + 2 * EDGE
    chunks = rows // 8
    any_space = pl.BlockSpec(memory_space=pl.ANY)
    turn = coriolis_rows(lax.axis_index("lat") * rows - EDGE, padded, rows * n_lat)
    turn = jnp.broadcast_to(turn[:, None], (padded, 128))
    dma = pltpu.SemaphoreType.DMA
    return pl.pallas_call(
        functools.partial(forecast_kernel, n_ens, n_lat),
        out_shape=jax.ShapeDtypeStruct(ensemble.shape, f32),
        in_specs=[
            any_space, pl.BlockSpec(memory_space=pltpu.SMEM), any_space, any_space,
            pl.BlockSpec(memory_space=pltpu.VMEM),
        ],
        out_specs=any_space,
        scratch_shapes=[
            *[pltpu.VMEM((2 * part_dev, fields, layers, 8, lon), f32) for _ in range(chunks)],
            pltpu.VMEM((part_dev, fields, layers, padded, wide), f32),
            pltpu.VMEM((part_dev, layers, padded, wide), f32),
            pltpu.VMEM((layers, padded, wide), f32),
            pltpu.VMEM((part_dev, SUBSTEPS, layers, padded, wide), f32),
            pltpu.VMEM(forcing.shape, forcing.dtype),
            pltpu.VMEM(depth.shape, f32),
            pltpu.VMEM((2, part_dev, fields, layers, 8, lon), f32),
            dma((2 * chunks,)), dma((2 * chunks,)), dma((chunks,)), dma((2,)), dma((6,)), dma((6,)), dma((2,)),
        ],
        compiler_params=pltpu.CompilerParams(
            collective_id=0, has_side_effects=True, vmem_limit_bytes=60 * 2**20
        ),
        name="forecast",
    )(ensemble, ancestors, depth, forcing, turn)


def solution(mesh):
    in_specs = (
        P("ens", None, None, "lat", None),
        P("ens"),
        P(None, "lat", None),
        P("ens", None, None, "lat", None),
    )
    out_specs = P("ens", None, None, "lat", None)
    return jax.shard_map(
        functools.partial(on_device, mesh.shape["ens"], mesh.shape["lat"]),
        mesh=mesh, in_specs=in_specs, out_specs=out_specs, check_vma=False,
    )
```

time: 309 us -> 140 us (0.45); the launches traced: 305 us -> 140 us
  Pallas kernels: 0 us -> 131 us
  waiting for transfers between devices: 123 us -> 0 us
  other arithmetic: 84 us -> 0.05 us
  local copies, waits for them, and re-layouts: 73.4 us -> 9.45 us
  starting transfers between devices: 23.8 us -> 0 us
    pallas_call x0 -> x1, Pallas kernels: none -> 131 us  [on_device(): pl.pallas_call(functools.partial(forecast_kernel, n_ens, n_lat), out_shap...]
    ppermute x10 -> x0, waiting for transfers between devices: 123 us -> none  [the longest x2 95.9 us: from_behind(): return lax.ppermute(block, axis, route)]
    slice x17 -> x0, local copies, waits for them, and re-layouts: 33.1 us -> none  [the longest x6 13.9 us: advance(): jnp.roll(inner_flux, -1, -1) - jnp.roll(inner_flux, 1, -1)]
    concatenate x4 -> x0, other arithmetic: 30.9 us -> none  [the longest x3 17.2 us: with_halo(): value = jnp.concatenate([before, value, after], axis=dim)]
    another operation x9 -> x0, other arithmetic: 24.6 us -> none  [the longest x6 23.1 us: advance(): jnp.stack([height_next[:, :, 1:band_rows + 1], east_next, north_next], ax...]
    ppermute x10 -> x0, starting transfers between devices: 23.8 us -> none  [the longest x4 14.7 us: with_halo(): before = lax.ppermute(last, axis, up)]
    squeeze x3 -> x0, local copies, waits for them, and re-layouts: 12.7 us -> none  [advance(): eastward = padded[:, 1]]
    gather x1 -> x0, local copies, waits for them, and re-layouts: 11.3 us -> none  [on_device(): chosen = jnp.take(window, position, axis=0)]
  transfers between devices with their start and end apart: 10 -> 0, of which waited for: 8 -> 0; matrix products, arithmetic and copies ran while one was open for 10% -> 0% of each run, Pallas kernels for 0% -> 0%
where the time goes in v2:
time: 140 us
  Pallas kernels  131 us (94%)
  local copies, waits for them, and re-layouts  9.45 us (7%)
    pallas_call x1, Pallas kernels, on_device(): pl.pallas_call(functools.partial(forecast_kernel, n_ens, n_lat), out_shap...  131 us
    unnamed x1, local copies, waits for them, and re-layouts  8.75 us

profile of v2, /device:TPU:0, one launch (start us, length us, event | category | flops | bytes accessed | tf_op | source)
XLA Modules:
  0.0 140.0 jit_solution(4772472473831227935)
XLA Ops:
  0.0 0.7 broadcast_in_dim.2.refs_4_
  0.8 130.5 %forecast.1 = f32[4,3,2,64,1440]{4,3,2,1,0:T(8,128)} custom-call(f32[4,3,2,64,1440]{4,3,2,1,0:T(8,128)} %refs_0_.1, s32[4]{0:T(128)} %refs_1_.1, f32[2,64,1440]{2,1,0:T(8,128)} %refs_2_.1, bf16[4,3,2,64,1440]{4,3,2,1,0:T(8,128)(2,1)} %refs_3_.1, f32[80,128]{1,0:T(8,128)} %broadcast_in_dim.2.refs_4_), custom_call_target="tpu_custom_call" | custom-call | tf_op jit(solution)/shard_map/forecast/pallas_call | solution.py:321
  131.3 8.7 %copy.6 = f32[4,3,2,64,1440]{4,3,2,1,0:T(8,128)} copy(f32[4,3,2,64,1440]{4,3,2,1,0:T(8,128)} %forecast.1) | data formatting | bytes 17694720
  (1 shorter events, 0.0 us)

commit v3 on v2

--- a/solution.py
+++ b/solution.py
@@ -209,87 +209,80 @@
         for c in to_hi:
             c.wait_recv()
 
-    def from_below(before, here):
-        return pltpu.roll(jnp.where(row == 7, before, here), 1, 0)
-
-    def from_above(after, here):
-        return pltpu.roll(jnp.where(row == 0, after, here), 7, 0)
-
-    def around(e):
-        inside = ((e > 0) | has_lo) & ((e < blocks - 1) | has_hi)
-        return at_block(e), at_block(jnp.maximum(e - 1, 0)), at_block(jnp.minimum(e + 1, blocks - 1)), inside
-
-    def heights_of(p, s, e):
-        here, before, after, inside = around(e)
+    def inside_of(e, c):
+        at = e * 8 + c + row
+        return ((at >= EDGE) | has_lo) & ((at < EDGE + rows) | has_hi)
+
+    def load(ref, index, e, c):
+        low = c % 8
+        return ref.at[(*index, pl.ds(pl.multiple_of((e + c // 8) * 8, 8), 16 if low else 8))][low : low + 8, :]
+
+    def save(ref, index, e, c, value):
+        low = c % 8
+        ref.at[(*index, pl.ds(pl.multiple_of((e + c // 8) * 8, 8), 16 if low else 8))][low : low + 8, :] = value
+
+    def heights_of(p, s, e, c):
         heights = []
         for k in range(layers):
-            east = deep[k, here, :] * state[p, 1, k, here, :]
-            north = deep[k, here, :] * state[p, 2, k, here, :]
-            below = from_below(deep[k, before, :] * state[p, 2, k, before, :], north)
-            above = from_above(deep[k, after, :] * state[p, 2, k, after, :], north)
+            east = load(deep, (k,), e, c) * load(state, (p, 1, k), e, c)
+            below = load(deep, (k,), e, c - 1) * load(state, (p, 2, k), e, c - 1)
+            above = load(deep, (k,), e, c + 1) * load(state, (p, 2, k), e, c + 1)
             divergence = (pltpu.roll(east, wide - 1, 1) - pltpu.roll(east, 1, 1)) * 0.5 + (above - below) * 0.5
-            height = state[p, 0, k, here, :] - time_step * divergence
+            height = load(state, (p, 0, k), e, c) - time_step * divergence
             heights.append(height)
-            state[p, 0, k, here, :] = height + force[p, s, k, here, :]
+            save(state, (p, 0, k), e, c, height + load(force, (p, s, k), e, c))
         base = functools.reduce(jnp.add, heights)
         lowered = jnp.zeros_like(base)
+        inside = inside_of(e, c)
         for k in range(layers):
             if k:
                 lowered = lowered + heights[k]
-            press[p, k, here, :] = jnp.where(inside, base + reduced_gravity * lowered, 0.0)
-
-    def velocities(p, e, final):
-        here, before, after, inside = around(e)
-        turn = jnp.concatenate([coriolis[here, :]] * (wide // 128), axis=1)
-        slot = lax.rem(e, 2)
-        for k in range(layers):
-            mid = press[p, k, here, :]
+            save(press, (p, k), e, c + 8, jnp.where(inside, base + reduced_gravity * lowered, 0.0))
+
+    def velocities(p, e, c):
+        inside = inside_of(e, c)
+        turn = jnp.concatenate([load(coriolis, (), e, c)] * (wide // 128), axis=1)
+        for k in range(layers):
+            mid = load(press, (p, k), e, c + 8)
             slope_east = (pltpu.roll(mid, wide - 1, 1) - pltpu.roll(mid, 1, 1)) * 0.5
-            slope_north = (from_above(press[p, k, after, :], mid) - from_below(press[p, k, before, :], mid)) * 0.5
-            north = state[p, 2, k, here, :]
-            east_next = state[p, 1, k, here, :] + time_step * (turn * north - slope_east)
+            slope_north = (load(press, (p, k), e, c + 9) - load(press, (p, k), e, c + 7)) * 0.5
+            north = load(state, (p, 2, k), e, c)
+            east_next = load(state, (p, 1, k), e, c) + time_step * (turn * north - slope_east)
             north_next = north + time_step * (-turn * east_next - slope_north)
-            if final:
-                stage_out[slot, p, 0, k, :, :] = state[p, 0, k, here, :][:, :lon]
-                stage_out[slot, p, 1, k, :, :] = east_next[:, :lon]
-                stage_out[slot, p, 2, k, :, :] = north_next[:, :lon]
-            else:
-                state[p, 1, k, here, :] = jnp.where(inside, east_next, 0.0)
-                state[p, 2, k, here, :] = jnp.where(inside, north_next, 0.0)
+            save(state, (p, 1, k), e, c, jnp.where(inside, east_next, 0.0))
+            save(state, (p, 2, k), e, c, jnp.where(inside, north_next, 0.0))
 
     def out_copy(e):
         slot = lax.rem(e, 2)
         return pltpu.make_async_copy(stage_out.at[slot], out.at[:, :, :, at_block(e - 1), :], out_sem.at[slot])
 
-    @pl.loop(0, blocks + 2 * SUBSTEPS - 2)
-    def _(step):
+    @pl.loop(0, blocks)
+    def _(e):
         for c in range(1, chunks - 1):
 
-            @pl.when(step == c)
+            @pl.when(e == c)
             def _():
                 take(c)
 
-        @pl.loop(0, SUBSTEPS)
-        def _(s):
-            e = step - 2 * s
-
-            @pl.when((e >= 0) & (e < blocks))
-            def _():
+        for s in range(SUBSTEPS):
+
+            def substep():
                 @pl.loop(0, part_dev)
                 def _(p):
-                    heights_of(p, s, e)
-
-            j = e - 1
-
-            @pl.when((j >= 0) & (j < blocks) & (s < SUBSTEPS - 1))
-            def _():
+                    heights_of(p, s, e, 3 - 2 * s)
+
                 @pl.loop(0, part_dev)
                 def _(p):
-                    velocities(p, j, False)
-
-        j = step - 2 * SUBSTEPS + 1
-
-        @pl.when((j >= 1) & (j < blocks - 1))
+                    velocities(p, e, 2 - 2 * s)
+
+            if s < 2:
+                substep()
+            else:
+                pl.when(e >= 1)(substep)
+
+        j = e - 1
+
+        @pl.when(j >= 1)
         def _():
             @pl.when(j >= 3)
             def _():
@@ -297,7 +290,9 @@
 
             @pl.loop(0, part_dev)
             def _(p):
-                velocities(p, j, True)
+                for f in range(3):
+                    for k in range(layers):
+                        stage_out[lax.rem(j, 2), p, f, k, :, :] = state[p, f, k, at_block(j), pl.ds(0, lon)]
 
             out_copy(j).start()
 
@@ -312,7 +307,7 @@
     part_dev, fields, layers, rows, lon = ensemble.shape
     f32 = jnp.float32
     wide = -(-lon // 128) * 128
-    padded = rows + 2 * EDGE
+    padded = rows + 3 * EDGE
     chunks = rows // 8
     any_space = pl.BlockSpec(memory_space=pl.ANY)
     turn = coriolis_rows(lax.axis_index("lat") * rows - EDGE, padded, rows * n_lat)
@@ -329,7 +324,7 @@
         scratch_shapes=[
             *[pltpu.VMEM((2 * part_dev, fields, layers, 8, lon), f32) for _ in range(chunks)],
             pltpu.VMEM((part_dev, fields, layers, padded, wide), f32),
-            pltpu.VMEM((part_dev, layers, padded, wide), f32),
+            pltpu.VMEM((part_dev, layers, padded + 8, wide), f32),
             pltpu.VMEM((layers, padded, wide), f32),
             pltpu.VMEM((part_dev, SUBSTEPS, layers, padded, wide), f32),
             pltpu.VMEM(forcing.shape, forcing.dtype),

time: 140 us -> 135 us (0.964)
  Pallas kernels: 131 us -> 125 us
    pallas_call x1, Pallas kernels: 131 us -> 125 us  [on_device(): pl.pallas_call(functools.partial(forecast_kernel, n_ens, n_lat), out_shap...]
where the time goes in v3:
time: 135 us
  Pallas kernels  125 us (93%)
  local copies, waits for them, and re-layouts  9.45 us (7%)
    pallas_call x1, Pallas kernels, on_device(): pl.pallas_call(functools.partial(forecast_kernel, n_ens, n_lat), out_shap...  125 us
    unnamed x1, local copies, waits for them, and re-layouts  8.75 us

profile of v3, /device:TPU:0, one launch (start us, length us, event | category | flops | bytes accessed | tf_op | source)
XLA Modules:
  0.0 135.0 jit_solution(11385339961035638696)
XLA Ops:
  0.0 0.7 broadcast_in_dim.2.refs_4_
  0.8 125.5 %forecast.1 = f32[4,3,2,64,1440]{4,3,2,1,0:T(8,128)} custom-call(f32[4,3,2,64,1440]{4,3,2,1,0:T(8,128)} %refs_0_.1, s32[4]{0:T(128)} %refs_1_.1, f32[2,64,1440]{2,1,0:T(8,128)} %refs_2_.1, bf16[4,3,2,64,1440]{4,3,2,1,0:T(8,128)(2,1)} %refs_3_.1, f32[88,128]{1,0:T(8,128)} %broadcast_in_dim.2.refs_4_), custom_call_target="tpu_custom_call" | custom-call | tf_op jit(solution)/shard_map/forecast/pallas_call | solution.py:316
  126.2 8.7 %copy.6 = f32[4,3,2,64,1440]{4,3,2,1,0:T(8,128)} copy(f32[4,3,2,64,1440]{4,3,2,1,0:T(8,128)} %forecast.1) | data formatting | bytes 17694720
  (1 shorter events, 0.0 us)

commit v4 on v3

--- a/solution.py
+++ b/solution.py
@@ -303,6 +303,10 @@
             copy.wait_send()
 
 
+def hand_over(source, target):
+    target[...] = source[...]
+
+
 def on_device(n_ens, n_lat, ensemble, ancestors, depth, forcing):
     part_dev, fields, layers, rows, lon = ensemble.shape
     f32 = jnp.float32
@@ -313,7 +317,7 @@
     turn = coriolis_rows(lax.axis_index("lat") * rows - EDGE, padded, rows * n_lat)
     turn = jnp.broadcast_to(turn[:, None], (padded, 128))
     dma = pltpu.SemaphoreType.DMA
-    return pl.pallas_call(
+    result = pl.pallas_call(
         functools.partial(forecast_kernel, n_ens, n_lat),
         out_shape=jax.ShapeDtypeStruct(ensemble.shape, f32),
         in_specs=[
@@ -337,6 +341,15 @@
         ),
         name="forecast",
     )(ensemble, ancestors, depth, forcing, turn)
+    block = pl.BlockSpec((1, 1, layers, rows, lon), lambda p, f: (p, f, 0, 0, 0))
+    return pl.pallas_call(
+        hand_over,
+        out_shape=jax.ShapeDtypeStruct(ensemble.shape, f32),
+        grid=(part_dev, fields),
+        in_specs=[block],
+        out_specs=block,
+        name="hand_over",
+    )(result)
 
 
 def solution(mesh):

time: 135 us -> 138 us (1.022)
  Pallas kernels: 125 us -> 137 us
  local copies, waits for them, and re-layouts: 9.45 us -> 0.7 us
    pallas_call x0 -> x1, Pallas kernels: none -> 11.5 us  [on_device(): pl.pallas_call(hand_over, out_shape=jax.ShapeDtypeStruct(ensemble.shape,...]
    unnamed x1 -> x0, local copies, waits for them, and re-layouts: 8.75 us -> none
where the time goes in v4:
time: 138 us
  Pallas kernels  137 us (99%)
    pallas_call x1, Pallas kernels, on_device(): pl.pallas_call(functools.partial(forecast_kernel, n_ens, n_lat), out_shap...  125 us
    pallas_call x1, Pallas kernels, on_device(): pl.pallas_call(hand_over, out_shape=jax.ShapeDtypeStruct(ensemble.shape,...  11.5 us

profile of v4, /device:TPU:0, one launch (start us, length us, event | category | flops | bytes accessed | tf_op | source)
XLA Modules:
  0.0 137.7 jit_solution(15125423964211508113)
XLA Ops:
  0.0 0.7 broadcast_in_dim.2.refs_4_
  0.8 125.5 %forecast.1.source = f32[4,3,2,64,1440]{4,3,2,1,0:T(8,128)} custom-call(f32[4,3,2,64,1440]{4,3,2,1,0:T(8,128)} %refs_0_.1, s32[4]{0:T(128)} %refs_1_.1, f32[2,64,1440]{2,1,0:T(8,128)} %refs_2_.1, bf16[4,3,2,64,1440]{4,3,2,1,0:T(8,128)(2,1)} %refs_3_.1, f32[88,128]{1,0:T(8,128)} %broadcast_in_dim.2.refs_4_), custom_call_target="tpu_custom_call" | custom-call | tf_op jit(solution)/shard_map/forecast/pallas_call | solution.py:320
  126.2 11.5 %hand_over.1 = f32[4,3,2,64,1440]{4,3,2,1,0:T(8,128)} custom-call(f32[4,3,2,64,1440]{4,3,2,1,0:T(8,128)} %forecast.1.source), custom_call_target="tpu_custom_call" | custom-call | tf_op jit(solution)/shard_map/hand_over/pallas_call | solution.py:345
  (1 shorter events, 0.0 us)
